TPU v7x, 256 devices: a whole 4x4x8 slice. The times are simulated.
256 devices in a mesh: row: 16 (over x, y_lo, core), col: 16 (over y_hi, z).
Axes of the slice: x: 4, y: 4 (y_hi: 2, y_lo: 2; y = y_hi * 2 + y_lo), z: 8, core: 2. Of those that a mesh axis runs over, the one named last changes fastest.
Arguments:
- design: bfloat16 [12288, 32768], P('row', 'col'), may hold values from -6 to 6
- species: int32 [12288], P('row'), may hold values from 0 to 9
- species_weight: float32 [10], replicated, may hold values from 0.2 to 5
Outputs:
- gram_tiles: float32 [32768, 2048], P(('col', 'row'))
All inputs are finite; a program needn't handle non-finite values.
Results may differ from a plain program's by a relative error of at most 0.0029.
Values may be sent and summed in bfloat16 or wider, within the bound.
A program may use at most 64 MiB of HBM per device.

v0:
```python
import jax
import jax.numpy as jnp
from jax import lax
from jax.sharding import PartitionSpec as P


def partner_2(value, axis, stride):
    mask = 2**stride
    pairs = [(source, source ^ mask) for source in range(lax.axis_size(axis))]
    return lax.ppermute(value, axis, pairs)


def shards(design, species, species_weight):
    row_count, block_width = design.shape
    onehot = (
        species[:, None] == jnp.arange(species_weight.shape[0], dtype=jnp.int32)[None, :]
    ).astype(jnp.float32)
    row_weight = jnp.sum(onehot * species_weight[None, :], axis=1)
    scaled = (design.astype(jnp.float32) * row_weight[:, None]).astype(jnp.bfloat16)
    row_devices = lax.axis_size("row")
    col_devices = lax.axis_size("col")
    normalizer = float(row_count * row_devices) ** (-0.5)
    bit_count = col_devices.bit_length() - 1
    bit_order = list(range(bit_count))
    partner = design
    for bit_index in bit_order:
        partner = partner_2(partner, "col", bit_index)
    gram_tile = lax.psum_scatter(
        lax.dot_general(
            scaled, partner, (((0,), (0,)), ((), ())), preferred_element_type=jnp.float32
        ),
        "row",
        scatter_dimension=0,
        tiled=True,
    )
    return gram_tile * normalizer


def solution(mesh):
    placed = (P("row", "col"), P("row"), P())
    return jax.shard_map(
        shards, mesh=mesh, in_specs=placed, out_specs=P(("col", "row"), None), check_vma=False
    )
```

profile of v0, /device:TPU:1, one launch (start us, length us, event | category | flops | bytes accessed | tf_op | source)
XLA Modules:
  0.0 632.5 jit_solution(15051169872163197851)
XLA Ops:
  6.5 0.0 reduce-scatter.2.cloned.1.call-start
  6.5 2.5 collective-permute-start
  9.0 67.1 %collective-permute-done = bf16[768,2048]{1,0:T(8,128)(2,1)S(1)} collective-permute-done((bf16[768,2048]{1,0:T(8,128)(2,1)}, bf16[768,2048]{1,0:T(8,128)(2,1)S(1)}, u32[]{:S(2)}, u32[]{:S(2)}) %collective-permute-start) | collective-permute-done | bytes 3145760 | tf_op jit(solution)/shard_map/ppermute | solution.py:10
  76.1 3.8 collective-permute-start.1
  79.9 134.9 %collective-permute-done.1 = bf16[768,2048]{1,0:T(8,128)(2,1)S(1)} collective-permute-done((bf16[768,2048]{1,0:T(8,128)(2,1)S(1)}, bf16[768,2048]{1,0:T(8,128)(2,1)S(1)}, u32[]{:S(2)}, u32[]{:S(2)}) %collective-permute-start.1) | collective-permute-done | bytes 3145760 | tf_op jit(solution)/shard_map/ppermute | solution.py:10
  214.8 6.4 %collective-permute-start.2 = (bf16[768,2048]{1,0:T(8,128)(2,1)S(1)}, bf16[768,2048]{1,0:T(8,128)(2,1)S(1)}, u32[]{:S(2)}, u32[]{:S(2)}) collective-permute-start(bf16[768,2048]{1,0:T(8,128)(2,1)S(1)} %collective-permute-done.1), channel_id=1, source_target_pairs={{0,4},{1,5},{2,6},{3,7},{4,0},{5,1},{6,2},{7,3},{8,12},{9,13},{10,... | collective-permute-start | bytes 9437192 | tf_op jit(solution)/shard_map/ppermute | solution.py:10
  221.3 135.6 %collective-permute-done.2 = bf16[768,2048]{1,0:T(8,128)(2,1)S(1)} collective-permute-done((bf16[768,2048]{1,0:T(8,128)(2,1)S(1)}, bf16[768,2048]{1,0:T(8,128)(2,1)S(1)}, u32[]{:S(2)}, u32[]{:S(2)}) %collective-permute-start.2) | collective-permute-done | bytes 3145760 | tf_op jit(solution)/shard_map/ppermute | solution.py:10
  356.8 2.9 collective-permute-start.3
  359.8 0.8 select_reduce_fusion
  360.5 65.7 %collective-permute-done.3 = bf16[768,2048]{1,0:T(8,128)(2,1)S(1)} collective-permute-done((bf16[768,2048]{1,0:T(8,128)(2,1)S(1)}, bf16[768,2048]{1,0:T(8,128)(2,1)S(1)}, u32[]{:S(2)}, u32[]{:S(2)}) %collective-permute-start.3) | collective-permute-done | bytes 3145760 | tf_op jit(solution)/shard_map/ppermute | solution.py:10
  426.3 12.5 %fusion = f32[2048,2048]{1,0:T(8,128)} fusion(bf16[768,2048]{1,0:T(8,128)(2,1)S(1)} %collective-permute-done.3, bf16[768,2048]{1,0:T(8,128)(2,1)} %param.3, f32[768]{0:T(1024)S(1)} %select_reduce_fusion), kind=kOutput, calls=%fused_computation.1 | convolution fusion | flops 6447169536 | bytes 23071744 | tf_op jit(solution)/shard_map/dot_general | solution.py:29
  438.7 0.0 reduce-scatter.2.cloned.1.call-update
  438.7 184.6 %reduce-scatter.2.cloned.1.call-done = f32[128,2048]{1,0:T(8,128)} async-done(((f32[2048,2048]{1,0:T(8,128)}), f32[128,2048]{1,0:T(8,128)}) %reduce-scatter.2.cloned.1.call-update) | async-done | bytes 1048592 | tf_op jit(solution)/shard_map/reduce_scatter | solution.py:28
  623.3 2.3 broadcast_multiply_fusion
Async XLA Ops:
  6.5 616.8 %reduce-scatter.2.cloned.1.call-start = ((), (), s32[]{:S(2)}) async-start(), calls=%async_computation.1 | async-start | bytes 17825792 | tf_op jit(solution)/shard_map/reduce_scatter | solution.py:28
  6.5 69.6 %collective-permute-start = (bf16[768,2048]{1,0:T(8,128)(2,1)}, bf16[768,2048]{1,0:T(8,128)(2,1)S(1)}, u32[]{:S(2)}, u32[]{:S(2)}) collective-permute-start(bf16[768,2048]{1,0:T(8,128)(2,1)} %param.3), channel_id=1, source_target_pairs={{0,1},{1,0},{2,3},{3,2},{4,5},{5,4},{6,7},{7,6},{8,9},{9,8},{10,11... | collective-permute-start | bytes 9437192 | tf_op jit(solution)/shard_map/ppermute | solution.py:10
  76.1 138.7 %collective-permute-start.1 = (bf16[768,2048]{1,0:T(8,128)(2,1)S(1)}, bf16[768,2048]{1,0:T(8,128)(2,1)S(1)}, u32[]{:S(2)}, u32[]{:S(2)}) collective-permute-start(bf16[768,2048]{1,0:T(8,128)(2,1)S(1)} %collective-permute-done), channel_id=1, source_target_pairs={{0,2},{1,3},{2,0},{3,1},{4,6},{5,7},{6,4},{7,5},{8,10},{9,11},{10,... | collective-permute-start | bytes 9437192 | tf_op jit(solution)/shard_map/ppermute | solution.py:10
  214.8 142.0 %collective-permute-start.2 = (bf16[768,2048]{1,0:T(8,128)(2,1)S(1)}, bf16[768,2048]{1,0:T(8,128)(2,1)S(1)}, u32[]{:S(2)}, u32[]{:S(2)}) collective-permute-start(bf16[768,2048]{1,0:T(8,128)(2,1)S(1)} %collective-permute-done.1), channel_id=1, source_target_pairs={{0,4},{1,5},{2,6},{3,7},{4,0},{5,1},{6,2},{7,3},{8,12},{9,13},{10,... | collective-permute-start | bytes 9437192 | tf_op jit(solution)/shard_map/ppermute | solution.py:10
  356.8 69.4 %collective-permute-start.3 = (bf16[768,2048]{1,0:T(8,128)(2,1)S(1)}, bf16[768,2048]{1,0:T(8,128)(2,1)S(1)}, u32[]{:S(2)}, u32[]{:S(2)}) collective-permute-start(bf16[768,2048]{1,0:T(8,128)(2,1)S(1)} %collective-permute-done.2), channel_id=1, source_target_pairs={{0,8},{1,9},{2,10},{3,11},{4,12},{5,13},{6,14},{7,15},{8,0},{9,1},... | collective-permute-start | bytes 9437192 | tf_op jit(solution)/shard_map/ppermute | solution.py:10
Sparse Core Ops, SparseCore 0:
  438.9 184.4 reduce-scatter.1
where the time goes:
time: 633 us; the launch traced here: 632 us
  waiting for transfers between devices  588 us (93%)
  starting transfers between devices  15.6 us (2%)
  between operations  13.4 us (2%)
  matrix products  12.5 us (2%)
    ppermute x4, waiting for transfers between devices, partner_2(): return lax.ppermute(value, axis, pairs)  403 us
    reduce_scatter x1, waiting for transfers between devices, shards(): lax.psum_scatter(lax.dot_general(scaled, partner, (((0,), (0,)), ((), ())...  185 us
    ppermute x4, starting transfers between devices, partner_2(): return lax.ppermute(value, axis, pairs)  15.6 us
  transfers between devices with their start and end apart: 5, of which 5 were waited for; matrix products, arithmetic and copies ran while one was open for 0% of the time, Pallas kernels for 0%

commit v1 on v0

v1 whole, which is shorter than its diff:
```python
import jax
import jax.numpy as jnp
from jax import lax
from jax.experimental import pallas as pl
from jax.experimental.pallas import tpu as pltpu
from jax.sharding import PartitionSpec as P

MESH = pl.DeviceIdType.MESH
BF = jnp.bfloat16
F32 = jnp.float32
DEPTH = 768
WIDTH = 2048
NB = 8
NORM = float(12288) ** -0.5


def kernel(
    design, weight, out,
    raw, wv, hi, lo, rbuf, rt, send_a, recv_a, own, send_b, recv_b, half, ret, tile,
    local_sem, ls, lr, ws, wr, rs, rr, as_, ar, bs, br, ts, tr, os_, orr,
):
    row = lax.axis_index("row")
    col = lax.axis_index("col")
    mirror = 15 - col
    core = lax.rem(row, 2)
    chip = lax.div(row, 2)
    y = lax.rem(chip, 2)
    x = lax.div(chip, 2)
    sibling = row + 1 - 2 * core
    across = row + 2 - 4 * y
    computes = lax.rem(col, 2) == 1
    barrier = pltpu.get_barrier_semaphore()

    def copy(src, dst, ss, rs_, to_row, to_col):
        return pltpu.make_async_remote_copy(
            src_ref=src, dst_ref=dst, send_sem=ss, recv_sem=rs_, device_id=(to_row, to_col), device_id_type=MESH
        )

    def greet(to_row, to_col):
        pl.semaphore_signal(barrier, inc=1, device_id=(to_row, to_col), device_id_type=MESH)

    def row_at(j):
        return lax.rem(x + j, 4) * 4 + y * 2 + core

    def design_copy(k, c):
        return copy(
            design.at[:, pl.ds(pl.multiple_of(k * 256 + c * 128, 128), 128)],
            rbuf.at[k, pl.ds(pl.multiple_of(core * DEPTH, DEPTH), DEPTH), :],
            rs.at[k, c], rr.at[k, core], chip * 2 + c, mirror,
        )

    def return_copy(k):
        return copy(
            ret.at[k], out.at[:, pl.ds(pl.multiple_of(chip * 256, 256), 256)], os_.at[k], orr.at[chip], 2 * k + core, mirror
        )

    @pl.when(jnp.logical_not(computes))
    def _():
        for q in range(8):
            greet(2 * q + core, mirror)
        pl.semaphore_wait(barrier, 2)

        def step(k, carry):
            for c in range(2):
                design_copy(k, c).start()

            @pl.when(k >= 2)
            def _():
                for c in range(2):
                    design_copy(k - 2, c).wait_send()

            return carry

        lax.fori_loop(0, NB, step, 0)
        for k in (NB - 2, NB - 1):
            for c in range(2):
                design_copy(k, c).wait_send()
        for q in range(8):
            copy(
                ret.at[0], out.at[:, pl.ds(q * 256, 256)], os_.at[0], orr.at[q], row, mirror
            ).wait_recv()

    @pl.when(computes)
    def _():
        greet(chip * 2, mirror)
        greet(chip * 2 + 1, mirror)
        greet(sibling, col)
        greet(across, col)
        for j in range(1, 4):
            greet(row_at(j), col)
        mine = pltpu.make_async_copy(design, raw.at[core], local_sem.at[0])
        mine_w = pltpu.make_async_copy(weight, wv.at[core], local_sem.at[1])
        mine.start()
        mine_w.start()
        pl.semaphore_wait(barrier, 13)
        theirs = copy(design, raw.at[core], ls, lr, sibling, col)
        theirs_w = copy(weight, wv.at[core], ws, wr, sibling, col)
        theirs_w.start()
        theirs.start()

        def scale(s):
            def piece(i, carry):
                at = pl.ds(pl.multiple_of(i * 32, 32), 32)
                to = pl.ds(pl.multiple_of(s * DEPTH + i * 32, 32), 32)
                value = raw[s, at, :].astype(F32) * wv[s, at, 0:1]
                high = value.astype(BF)
                hi[to, :] = high
                lo[to, :] = (value - high.astype(F32)).astype(BF)
                return carry

            lax.fori_loop(0, DEPTH // 32, piece, 0)

        mine.wait()
        mine_w.wait()
        scale(core)
        theirs_w.wait()
        theirs.wait()
        scale(1 - core)

        def copy_a(k, j):
            return copy(send_a.at[k, j - 1], recv_a.at[k, j - 1], as_.at[k, j - 1], ar.at[k, j - 1], row_at(j), col)

        def copy_b(k):
            return copy(send_b.at[k], recv_b.at[k], bs.at[k], br.at[k], across, col)

        def copy_t(k):
            return copy(
                tile.at[k], out.at[:, pl.ds(pl.multiple_of(k * 256 + core * 128, 128), 128)], ts.at[k], tr.at[k], sibling, col
            )

        def multiply(k):
            for c in range(2):
                copy(
                    design.at[:, pl.ds(0, 128)], rbuf.at[k, pl.ds(c * DEPTH, DEPTH), :], rs.at[k, c], rr.at[k, c], row, mirror
                ).wait_recv()
            rt[...] = rbuf[k].T
            for j in (2, 1, 3, 0):
                at = pl.ds(pl.multiple_of(lax.rem(x + j, 4) * 512, 512), 512)
                part = jnp.dot(rt[...], hi[:, at], preferred_element_type=F32)
                part += jnp.dot(rt[...], lo[:, at], preferred_element_type=F32)
                if j:
                    send_a[k, j - 1] = part.astype(BF)
                    copy_a(k, j).start()
                else:
                    own[k] = part

        def sum_x(k):
            for j in range(1, 4):
                copy_a(k, j).wait_recv()
            at_mine = pl.ds(pl.multiple_of(y * 256, 256), 256)
            at_other = pl.ds(pl.multiple_of(256 - y * 256, 256), 256)

            def total(at):
                t = own[k, :, at]
                for j in range(3):
                    t += recv_a[k, j, :, at].astype(F32)
                return t

            send_b[k] = total(at_other)
            copy_b(k).start()
            half[k] = total(at_mine)

        def sum_y(k):
            copy_b(k).wait_recv()
            ret[k] = (half[k] + recv_b[k]) * NORM
            return_copy(k).start()
            tile[k] = ret[k, :, pl.ds(pl.multiple_of(128 - core * 128, 128), 128)].T
            copy_t(k).start()
            out[:, pl.ds(pl.multiple_of(k * 256 + core * 128, 128), 128)] = ret[
                k, :, pl.ds(pl.multiple_of(core * 128, 128), 128)
            ].T

        def step(k, carry):
            multiply(k)

            @pl.when(k >= 1)
            def _():
                sum_x(k - 1)

            @pl.when(k >= 2)
            def _():
                sum_y(k - 2)

            return carry

        lax.fori_loop(0, NB, step, 0)
        sum_x(NB - 1)
        sum_y(NB - 2)
        sum_y(NB - 1)

        def finish(k, carry):
            for j in range(1, 4):
                copy_a(k, j).wait_send()
            copy_b(k).wait_send()
            return_copy(k).wait_send()
            copy_t(k).wait_send()
            copy(
                tile.at[k], out.at[:, pl.ds(pl.multiple_of(k * 256 + 128 - core * 128, 128), 128)],
                ts.at[k], tr.at[k], sibling, col,
            ).wait_recv()
            return carry

        lax.fori_loop(0, NB, finish, 0)


def shards(design, species, species_weight):
    onehot = (
        species[:, None] == jnp.arange(species_weight.shape[0], dtype=jnp.int32)[None, :]
    ).astype(jnp.float32)
    row_weight = jnp.sum(onehot * species_weight[None, :], axis=1)
    weight = jnp.broadcast_to(row_weight[:, None], (DEPTH, 128))
    dma = pltpu.SemaphoreType.DMA
    vmem = pltpu.VMEM
    return pl.pallas_call(
        kernel,
        out_shape=jax.ShapeDtypeStruct((128, WIDTH), F32),
        in_specs=[pl.BlockSpec(memory_space=pl.ANY)] * 2,
        out_specs=pl.BlockSpec(memory_space=pltpu.VMEM),
        scratch_shapes=[
            vmem((2, DEPTH, WIDTH), BF),
            vmem((2, DEPTH, 128), F32),
            vmem((2 * DEPTH, WIDTH), BF),
            vmem((2 * DEPTH, WIDTH), BF),
            vmem((NB, 2 * DEPTH, 128), BF),
            vmem((128, 2 * DEPTH), BF),
            vmem((NB, 3, 128, 512), BF),
            vmem((NB, 3, 128, 512), BF),
            vmem((NB, 128, 512), F32),
            vmem((NB, 128, 256), F32),
            vmem((NB, 128, 256), F32),
            vmem((NB, 128, 256), F32),
            vmem((NB, 128, 256), F32),
            vmem((NB, 128, 128), F32),
            dma((2,)),
            dma, dma, dma, dma,
            dma((NB, 2)), dma((NB, 2)),
            dma((NB, 3)), dma((NB, 3)),
            dma((NB,)), dma((NB,)),
            dma((NB,)), dma((NB,)),
            dma((NB,)), dma((8,)),
        ],
        compiler_params=pltpu.CompilerParams(
            collective_id=0, has_side_effects=True, vmem_limit_bytes=56 * 2**20
        ),
        cost_estimate=pl.CostEstimate(flops=4 * 1536 * 2048 * 1024, bytes_accessed=8 * 2**20, transcendentals=0),
    )(design, weight)


def solution(mesh):
    placed = (P("row", "col"), P("row"), P())
    return jax.shard_map(
        shards, mesh=mesh, in_specs=placed, out_specs=P(("col", "row"), None), check_vma=False
    )
```

time: 633 us -> 152 us (0.24)
  the two profiles are of different devices: /device:TPU:1 before, /device:TPU:94 now
where the time goes in v1:
time: 152 us; the launch traced here: 151 us
  Pallas kernels  147 us (97%)
  local copies, waits for them, and re-layouts  3.21 us (2%)
    pallas_call x1, Pallas kernels, shards(): pl.pallas_call(kernel, out_shape=jax.ShapeDtypeStruct((128, WIDTH), F32),...  147 us

profile of v1, /device:TPU:94, one launch (start us, length us, event | category | flops | bytes accessed | tf_op | source)
XLA Modules:
  0.0 151.4 jit_solution(12856429118104052417)
XLA Ops:
  0.0 0.8 select_reduce_fusion
  0.8 0.9 broadcast_in_dim.2.weight
  1.7 147.4 %shard_map.37 = f32[128,2048]{1,0:T(8,128)} custom-call(bf16[768,2048]{1,0:T(8,128)(2,1)} %design.1, f32[768,128]{1,0:T(8,128)} %broadcast_in_dim.2.weight), custom_call_target="tpu_custom_call" | custom-call | flops 12884901888 | bytes 8388608 | tf_op jit(solution)/shard_map/pallas_call | solution.py:214
  149.1 2.3 %copy.5 = f32[128,2048]{1,0:T(8,128)} copy(f32[128,2048]{1,0:T(8,128)} %shard_map.37) | data formatting | bytes 2097152

commit v2 on v1

--- a/solution.py
+++ b/solution.py
@@ -16,12 +16,13 @@
 
 def kernel(
     design, weight, out,
-    raw, wv, hi, lo, rbuf, rt, send_a, recv_a, own, send_b, recv_b, half, ret, tile,
-    local_sem, ls, lr, ws, wr, rs, rr, as_, ar, bs, br, ts, tr, os_, orr,
+    raw, wv, hi, lo, rbuf, rt, send_a, recv_a, own, send_b, recv_b, half, ret, tile, stage, recv_q,
+    local_sem, ls, lr, ws, wr, rs, rr, as_, ar, bs, br, ts, tr, os_, orr, gs, gr,
 ):
     row = lax.axis_index("row")
     col = lax.axis_index("col")
     mirror = 15 - col
+    beside = lax.rem(col + 8, 16)
     core = lax.rem(row, 2)
     chip = lax.div(row, 2)
     y = lax.rem(chip, 2)
@@ -49,41 +50,72 @@
             rs.at[k, c], rr.at[k, core], chip * 2 + c, mirror,
         )
 
+    def stage_copy(i, c):
+        return copy(
+            design.at[:, pl.ds(pl.multiple_of((2 * i + 1) * 256 + c * 128, 128), 128)],
+            stage.at[i, c], gs.at[i, c], gr.at[i, c], row, beside,
+        )
+
+    def forward_copy(i, c):
+        return copy(
+            stage.at[i, c], rbuf.at[2 * i + 1, pl.ds(pl.multiple_of(core * DEPTH, DEPTH), DEPTH), :],
+            rs.at[2 * i + 1, c], rr.at[2 * i + 1, core], chip * 2 + c, 15 - beside,
+        )
+
     def return_copy(k):
-        return copy(
-            ret.at[k], out.at[:, pl.ds(pl.multiple_of(chip * 256, 256), 256)], os_.at[k], orr.at[chip], 2 * k + core, mirror
-        )
+        return copy(ret.at[k], recv_q.at[chip], os_.at[k], orr.at[chip], 2 * k + core, mirror)
 
     @pl.when(jnp.logical_not(computes))
     def _():
         for q in range(8):
             greet(2 * q + core, mirror)
-        pl.semaphore_wait(barrier, 2)
-
-        def step(k, carry):
+        greet(row, beside)
+        pl.semaphore_wait(barrier, 5)
+        for c in range(2):
+            stage_copy(0, c).start()
+        for c in range(2):
+            design_copy(0, c).start()
+
+        def step(i, carry):
+            @pl.when(i < NB // 2 - 1)
+            def _():
+                for c in range(2):
+                    stage_copy(i + 1, c).start()
+
             for c in range(2):
-                design_copy(k, c).start()
-
-            @pl.when(k >= 2)
+                stage_copy(i, c).wait_recv()
+                forward_copy(i, c).start()
+
+            @pl.when(i < NB // 2 - 1)
             def _():
                 for c in range(2):
-                    design_copy(k - 2, c).wait_send()
+                    design_copy(2 * i + 2, c).start()
+
+            for c in range(2):
+                stage_copy(i, c).wait_send()
+                design_copy(2 * i, c).wait_send()
+
+            @pl.when(i >= 1)
+            def _():
+                for c in range(2):
+                    forward_copy(i - 1, c).wait_send()
 
             return carry
 
-        lax.fori_loop(0, NB, step, 0)
-        for k in (NB - 2, NB - 1):
-            for c in range(2):
-                design_copy(k, c).wait_send()
+        lax.fori_loop(0, NB // 2, step, 0)
+        for c in range(2):
+            forward_copy(NB // 2 - 1, c).wait_send()
         for q in range(8):
-            copy(
-                ret.at[0], out.at[:, pl.ds(q * 256, 256)], os_.at[0], orr.at[q], row, mirror
-            ).wait_recv()
+            copy(ret.at[0], recv_q.at[q], os_.at[0], orr.at[q], row, mirror).wait_recv()
+            size = jnp.exp2(recv_q[q, 128:144, :].astype(F32)[0:1, :] - 15.0)
+            out[:, q * 256 : q * 256 + 256] = recv_q[q, 0:128, :].astype(F32) * size
 
     @pl.when(computes)
     def _():
         greet(chip * 2, mirror)
         greet(chip * 2 + 1, mirror)
+        for c in range(2):
+            greet(chip * 2 + c, lax.rem(mirror + 8, 16))
         greet(sibling, col)
         greet(across, col)
         for j in range(1, 4):
@@ -162,11 +194,17 @@
 
         def sum_y(k):
             copy_b(k).wait_recv()
-            ret[k] = (half[k] + recv_b[k]) * NORM
+            done = (half[k] + recv_b[k]) * NORM
+            half[k] = done
+            largest = jnp.max(jnp.max(jnp.abs(done), axis=0, keepdims=True), axis=1, keepdims=True)
+            power = jnp.maximum(jnp.ceil(jnp.log2(jnp.maximum(largest, 1e-30))), -99.0)
+            steps = jnp.clip(jnp.round(done * jnp.exp2(15.0 - power)), -32767.0, 32767.0)
+            ret[k, 0:128, :] = steps.astype(jnp.int32).astype(jnp.int16)
+            ret[k, 128:144, :] = jnp.broadcast_to(power, (16, 256)).astype(jnp.int32).astype(jnp.int16)
             return_copy(k).start()
-            tile[k] = ret[k, :, pl.ds(pl.multiple_of(128 - core * 128, 128), 128)].T
+            tile[k] = half[k, :, pl.ds(pl.multiple_of(128 - core * 128, 128), 128)].T
             copy_t(k).start()
-            out[:, pl.ds(pl.multiple_of(k * 256 + core * 128, 128), 128)] = ret[
+            out[:, pl.ds(pl.multiple_of(k * 256 + core * 128, 128), 128)] = half[
                 k, :, pl.ds(pl.multiple_of(core * 128, 128), 128)
             ].T
 
@@ -229,8 +267,10 @@
             vmem((NB, 128, 256), F32),
             vmem((NB, 128, 256), F32),
             vmem((NB, 128, 256), F32),
-            vmem((NB, 128, 256), F32),
+            vmem((NB, 144, 256), jnp.int16),
             vmem((NB, 128, 128), F32),
+            vmem((NB // 2, 2, DEPTH, 128), BF),
+            vmem((8, 144, 256), jnp.int16),
             dma((2,)),
             dma, dma, dma, dma,
             dma((NB, 2)), dma((NB, 2)),
@@ -238,6 +278,7 @@
             dma((NB,)), dma((NB,)),
             dma((NB,)), dma((NB,)),
             dma((NB,)), dma((8,)),
+            dma((NB // 2, 2)), dma((NB // 2, 2)),
         ],
         compiler_params=pltpu.CompilerParams(
             collective_id=0, has_side_effects=True, vmem_limit_bytes=56 * 2**20

time: 152 us -> 118 us (0.78)
  the two profiles are of different devices: /device:TPU:94 before, /device:TPU:15 now
where the time goes in v2:
time: 118 us; the launch traced here: 117 us
  Pallas kernels  113 us (96%)
  local copies, waits for them, and re-layouts  3.21 us (3%)
    pallas_call x1, Pallas kernels, shards(): pl.pallas_call(kernel, out_shape=jax.ShapeDtypeStruct((128, WIDTH), F32),...  113 us

profile of v2, /device:TPU:15, one launch (start us, length us, event | category | flops | bytes accessed | tf_op | source)
XLA Modules:
  0.0 117.4 jit_solution(12033913124231223898)
XLA Ops:
  0.0 0.8 select_reduce_fusion
  0.8 0.9 broadcast_in_dim.2.weight
  1.7 113.4 %shard_map.37 = f32[128,2048]{1,0:T(8,128)} custom-call(bf16[768,2048]{1,0:T(8,128)(2,1)} %design.1, f32[768,128]{1,0:T(8,128)} %broadcast_in_dim.2.weight), custom_call_target="tpu_custom_call" | custom-call | flops 12884901888 | bytes 8388608 | tf_op jit(solution)/shard_map/pallas_call | solution.py:252
  115.1 2.3 %copy.5 = f32[128,2048]{1,0:T(8,128)} copy(f32[128,2048]{1,0:T(8,128)} %shard_map.37) | data formatting | bytes 2097152

commit v3 on v2

--- a/solution.py
+++ b/solution.py
@@ -15,8 +15,8 @@
 
 
 def kernel(
-    design, weight, out,
-    raw, wv, hi, lo, rbuf, rt, send_a, recv_a, own, send_b, recv_b, half, ret, tile, stage, recv_q,
+    design, species, species_weight, out,
+    raw, wv, hi, lo, rbuf, rt, send_a, recv_a, own, send_b, recv_b, half, ret, tile, stage, recv_q, species_here, weight_here,
     local_sem, ls, lr, ws, wr, rs, rr, as_, ar, bs, br, ts, tr, os_, orr, gs, gr,
 ):
     row = lax.axis_index("row")
@@ -121,12 +121,22 @@
         for j in range(1, 4):
             greet(row_at(j), col)
         mine = pltpu.make_async_copy(design, raw.at[core], local_sem.at[0])
-        mine_w = pltpu.make_async_copy(weight, wv.at[core], local_sem.at[1])
         mine.start()
-        mine_w.start()
+        kinds = pltpu.make_async_copy(species, species_here, local_sem.at[1])
+        kinds.start()
+        by_kind = pltpu.make_async_copy(species_weight, weight_here, local_sem.at[2])
+        by_kind.start()
+        kinds.wait()
+        by_kind.wait()
+        for i in range(DEPTH // 128):
+            kind = species_here[i * 128 : i * 128 + 128].reshape(1, 128)
+            value = jnp.zeros((1, 128), F32)
+            for n in range(10):
+                value = jnp.where(kind == n, weight_here[n], value)
+            wv[core, i * 128 : i * 128 + 128, :] = jnp.broadcast_to(value, (128, 128)).T
         pl.semaphore_wait(barrier, 13)
         theirs = copy(design, raw.at[core], ls, lr, sibling, col)
-        theirs_w = copy(weight, wv.at[core], ws, wr, sibling, col)
+        theirs_w = copy(wv.at[core], wv.at[core], ws, wr, sibling, col)
         theirs_w.start()
         theirs.start()
 
@@ -143,7 +153,6 @@
             lax.fori_loop(0, DEPTH // 32, piece, 0)
 
         mine.wait()
-        mine_w.wait()
         scale(core)
         theirs_w.wait()
         theirs.wait()
@@ -192,7 +201,7 @@
             copy_b(k).start()
             half[k] = total(at_mine)
 
-        def sum_y(k):
+        def sum_y(k, now=False):
             copy_b(k).wait_recv()
             done = (half[k] + recv_b[k]) * NORM
             half[k] = done
@@ -201,7 +210,8 @@
             steps = jnp.clip(jnp.round(done * jnp.exp2(15.0 - power)), -32767.0, 32767.0)
             ret[k, 0:128, :] = steps.astype(jnp.int32).astype(jnp.int16)
             ret[k, 128:144, :] = jnp.broadcast_to(power, (16, 256)).astype(jnp.int32).astype(jnp.int16)
-            return_copy(k).start()
+            if now:
+                return_copy(k).start()
             tile[k] = half[k, :, pl.ds(pl.multiple_of(128 - core * 128, 128), 128)].T
             copy_t(k).start()
             out[:, pl.ds(pl.multiple_of(k * 256 + core * 128, 128), 128)] = half[
@@ -222,9 +232,11 @@
             return carry
 
         lax.fori_loop(0, NB, step, 0)
+        for i in range(NB - 2):
+            return_copy(lax.rem(chip + i, NB - 2)).start()
         sum_x(NB - 1)
-        sum_y(NB - 2)
-        sum_y(NB - 1)
+        sum_y(NB - 2, True)
+        sum_y(NB - 1, True)
 
         def finish(k, carry):
             for j in range(1, 4):
@@ -242,17 +254,12 @@
 
 
 def shards(design, species, species_weight):
-    onehot = (
-        species[:, None] == jnp.arange(species_weight.shape[0], dtype=jnp.int32)[None, :]
-    ).astype(jnp.float32)
-    row_weight = jnp.sum(onehot * species_weight[None, :], axis=1)
-    weight = jnp.broadcast_to(row_weight[:, None], (DEPTH, 128))
     dma = pltpu.SemaphoreType.DMA
     vmem = pltpu.VMEM
     return pl.pallas_call(
         kernel,
         out_shape=jax.ShapeDtypeStruct((128, WIDTH), F32),
-        in_specs=[pl.BlockSpec(memory_space=pl.ANY)] * 2,
+        in_specs=[pl.BlockSpec(memory_space=pltpu.HBM)] * 3,
         out_specs=pl.BlockSpec(memory_space=pltpu.VMEM),
         scratch_shapes=[
             vmem((2, DEPTH, WIDTH), BF),
@@ -271,7 +278,9 @@
             vmem((NB, 128, 128), F32),
             vmem((NB // 2, 2, DEPTH, 128), BF),
             vmem((8, 144, 256), jnp.int16),
-            dma((2,)),
+            vmem((DEPTH,), jnp.int32),
+            pltpu.SMEM((10,), F32),
+            dma((3,)),
             dma, dma, dma, dma,
             dma((NB, 2)), dma((NB, 2)),
             dma((NB, 3)), dma((NB, 3)),
@@ -281,10 +290,10 @@
             dma((NB // 2, 2)), dma((NB // 2, 2)),
         ],
         compiler_params=pltpu.CompilerParams(
-            collective_id=0, has_side_effects=True, vmem_limit_bytes=56 * 2**20
+            collective_id=0, has_side_effects=True, vmem_limit_bytes=50 * 2**20
         ),
         cost_estimate=pl.CostEstimate(flops=4 * 1536 * 2048 * 1024, bytes_accessed=8 * 2**20, transcendentals=0),
-    )(design, weight)
+    )(*(pltpu.with_memory_space_constraint(a, pltpu.HBM) for a in (design, species, species_weight)))
 
 
 def solution(mesh):

time: 118 us -> 105 us (0.89)
  the two profiles are of different devices: /device:TPU:15 before, /device:TPU:95 now
where the time goes in v3:
time: 105 us
  Pallas kernels  104 us (99%)
    pallas_call x1, Pallas kernels, shards(): pl.pallas_call(kernel, out_shape=jax.ShapeDtypeStruct((128, WIDTH), F32),...  104 us

profile of v3, /device:TPU:95, one launch (start us, length us, event | category | flops | bytes accessed | tf_op | source)
XLA Modules:
  0.0 104.9 jit_solution(12212135407950272210)
XLA Ops:
  0.0 103.9 %shard_map.37 = f32[128,2048]{1,0:T(8,128)S(1)} custom-call(bf16[768,2048]{1,0:T(8,128)(2,1)} %design.1, s32[768]{0:T(1024)} %species.1, f32[10]{0:T(128)} %species_weight.1), custom_call_target="tpu_custom_call" | custom-call | flops 12884901888 | bytes 8388608 | tf_op jit(solution)/shard_map/pallas_call | solution.py:259
  103.9 1.0 copy.5

commit v4 on v3

v4 whole, which is shorter than its diff:
```python
import jax
import jax.numpy as jnp
from jax import lax
from jax.experimental import pallas as pl
from jax.experimental.pallas import tpu as pltpu
from jax.sharding import PartitionSpec as P

MESH = pl.DeviceIdType.MESH
BF = jnp.bfloat16
F32 = jnp.float32
DEPTH = 768
WIDTH = 2048
NB = 8
LAST = NB - 1
NORM = float(12288) ** -0.5


def kernel(
    design, species, species_weight, out,
    raw, wv, hi, lo, rbuf, rt, send_a, recv_a, own, send_b, recv_b, half, ret, tile, stage, recv_q, species_here, weight_here,
    mix, gathered, ret_last, send_d, recv_d,
    local_sem, ls, lr, ws, wr, rs, rr, as_, ar, bs, br, ts, tr, os_, orr, gs, gr, ds_, dr, fs, fr,
):
    row = lax.axis_index("row")
    col = lax.axis_index("col")
    mirror = 15 - col
    beside = lax.rem(col + 8, 16)
    core = lax.rem(row, 2)
    chip = lax.div(row, 2)
    y = lax.rem(chip, 2)
    x = lax.div(chip, 2)
    sibling = row + 1 - 2 * core
    across = row + 2 - 4 * y
    computes = lax.rem(col, 2) == 1
    barrier = pltpu.get_barrier_semaphore()

    def copy(src, dst, ss, rs_, to_row, to_col):
        return pltpu.make_async_remote_copy(
            src_ref=src, dst_ref=dst, send_sem=ss, recv_sem=rs_, device_id=(to_row, to_col), device_id_type=MESH
        )

    def greet(to_row, to_col):
        pl.semaphore_signal(barrier, inc=1, device_id=(to_row, to_col), device_id_type=MESH)

    def chip_at(j, d):
        return lax.rem(x + j, 4) * 2 + lax.rem(y + d, 2)

    mine_128 = pl.ds(pl.multiple_of(core * 128, 128), 128)
    other_128 = pl.ds(pl.multiple_of(128 - core * 128, 128), 128)
    my_rows = pl.ds(pl.multiple_of(core * DEPTH, DEPTH), DEPTH)

    def design_copy(k, c):
        return copy(mix.at[k, c], rbuf.at[k, my_rows, :], rs.at[k, c], rr.at[k, core], chip * 2 + c, mirror)

    def stage_copy(i, c):
        return copy(mix.at[2 * i + 1, c], stage.at[i, c], gs.at[i, c], gr.at[i, c], row, beside)

    def forward_copy(i, c):
        k = 2 * i + 1
        return copy(stage.at[i, c], rbuf.at[k, my_rows, :], rs.at[k, c], rr.at[k, core], chip * 2 + c, 15 - beside)

    def return_copy(q):
        return copy(ret.at[q], recv_q.at[chip, pl.ds(0, 112), :], os_.at[q], orr.at[chip], 2 * q + core, mirror)

    def return_last(q):
        return copy(ret_last.at[q], recv_q.at[chip, pl.ds(112, 48), :], fs.at[q], fr.at[chip], 2 * q + core, mirror)

    @pl.when(jnp.logical_not(computes))
    def _():
        for q in range(8):
            greet(2 * q + core, mirror)
        greet(row, beside)
        here = pltpu.make_async_copy(design, raw.at[0], local_sem.at[0])
        here.start()

        def mixing(k, carry):
            a = lax.broadcasted_iota(jnp.int32, (1024, 128), 0)
            b = lax.broadcasted_iota(jnp.int32, (1024, 128), 1)
            wanted = lax.div(b, 16) * 128 + k * 16 + lax.rem(b, 16)
            order = jnp.where(a == wanted, 1.0, 0.0).astype(BF)
            for c in range(2):
                found = jnp.concatenate([raw[0, :, q * 256 + c * 128 : q * 256 + c * 128 + 128] for q in range(8)], axis=1)
                mix[k, c] = jnp.dot(found, order, preferred_element_type=F32).astype(BF)
            return carry

        here.wait()
        lax.fori_loop(0, 2, mixing, 0)
        pl.semaphore_wait(barrier, 5)
        for c in range(2):
            stage_copy(0, c).start()
        for c in range(2):
            design_copy(0, c).start()
        lax.fori_loop(2, 4, mixing, 0)
        for c in range(2):
            stage_copy(1, c).start()
        lax.fori_loop(4, NB, mixing, 0)

        for i in range(NB // 2):
            if 1 <= i < NB // 2 - 1:
                for c in range(2):
                    stage_copy(i + 1, c).start()
            for c in range(2):
                stage_copy(i, c).wait_recv()
                forward_copy(i, c).start()
            if i < NB // 2 - 1:
                for c in range(2):
                    design_copy(2 * i + 2, c).start()
            for c in range(2):
                stage_copy(i, c).wait_send()
                design_copy(2 * i, c).wait_send()
                if i >= 1:
                    forward_copy(i - 1, c).wait_send()
        for c in range(2):
            forward_copy(NB // 2 - 1, c).wait_send()

        def unpack(q, rows, first, to):
            size = jnp.exp2(recv_q[q, first + rows : first + rows + 16, :].astype(F32)[0:1, :] - 15.0)
            out[to : to + rows, q * 256 : q * 256 + 256] = recv_q[q, first : first + rows, :].astype(F32) * size

        for q in range(8):
            copy(ret.at[0], recv_q.at[q, pl.ds(0, 112), :], os_.at[0], orr.at[q], row, mirror).wait_recv()
            unpack(q, 96, 0, 0)
        for q in range(8):
            copy(ret_last.at[0], recv_q.at[q, pl.ds(112, 48), :], fs.at[0], fr.at[q], row, mirror).wait_recv()
            unpack(q, 32, 112, 96)

    @pl.when(computes)
    def _():
        for c in range(2):
            greet(chip * 2 + c, mirror)
        for c in range(2):
            greet(chip * 2 + c, lax.rem(mirror + 8, 16))
        greet(sibling, col)
        for n in range(1, 8):
            greet(chip_at(n // 2, n % 2) * 2 + core, col)
        mine = pltpu.make_async_copy(design, raw.at[core], local_sem.at[0])
        mine.start()
        kinds = pltpu.make_async_copy(species, species_here, local_sem.at[1])
        kinds.start()
        by_kind = pltpu.make_async_copy(species_weight, weight_here, local_sem.at[2])
        by_kind.start()
        kinds.wait()
        by_kind.wait()
        for i in range(DEPTH // 128):
            kind = species_here[i * 128 : i * 128 + 128].reshape(1, 128)
            value = jnp.zeros((1, 128), F32)
            for n in range(10):
                value = jnp.where(kind == n, weight_here[n], value)
            wv[core, i * 128 : i * 128 + 128, :] = jnp.broadcast_to(value, (128, 128)).T
        pl.semaphore_wait(barrier, 16)
        theirs = copy(design, raw.at[core], ls, lr, sibling, col)
        theirs_w = copy(wv.at[core], wv.at[core], ws, wr, sibling, col)
        theirs_w.start()
        theirs.start()

        def scale(s):
            def some(i, carry):
                at = pl.ds(pl.multiple_of(i * 32, 32), 32)
                to = pl.ds(pl.multiple_of(s * DEPTH + i * 32, 32), 32)
                value = raw[s, at, :].astype(F32) * wv[s, at, 0:1]
                high = value.astype(BF)
                hi[to, :] = high
                lo[to, :] = (value - high.astype(F32)).astype(BF)
                return carry

            lax.fori_loop(0, DEPTH // 32, some, 0)

        mine.wait()
        scale(core)
        theirs_w.wait()
        theirs.wait()
        scale(1 - core)

        def copy_a(k, j):
            return copy(
                send_a.at[k, j - 1], recv_a.at[k, j - 1], as_.at[k, j - 1], ar.at[k, j - 1], chip_at(j, 0) * 2 + core, col
            )

        def copy_b(k):
            return copy(send_b.at[k], recv_b.at[k], bs.at[k], br.at[k], across, col)

        def copy_d(n):
            return copy(
                send_d.at[n - 1], recv_d.at[n - 1], ds_.at[n - 1], dr.at[n - 1], chip_at(n // 2, n % 2) * 2 + core, col
            )

        def copy_t(q, c):
            return copy(
                tile.at[q], out.at[:, pl.ds(pl.multiple_of(q * 256 + c * 128, 128), 128)], ts.at[q], tr.at[q], sibling, col
            )

        def arrived(k):
            for c in range(2):
                copy(
                    mix.at[k, c], rbuf.at[k, pl.ds(c * DEPTH, DEPTH), :], rs.at[k, c], rr.at[k, c], row, mirror
                ).wait_recv()
            rt[...] = rbuf[k].T

        def product(at):
            part = jnp.dot(rt[...], hi[:, at], preferred_element_type=F32)
            return part + jnp.dot(rt[...], lo[:, at], preferred_element_type=F32)

        def multiply(k):
            arrived(k)
            for j in (2, 1, 3, 0):
                part = product(pl.ds(pl.multiple_of(lax.rem(x + j, 4) * 512, 512), 512))
                if j:
                    send_a[k, j - 1] = part.astype(BF)
                    copy_a(k, j).start()
                else:
                    own[k] = part

        def sum_x(k):
            for j in range(1, 4):
                copy_a(k, j).wait_recv()
            at_mine = pl.ds(pl.multiple_of(y * 256, 256), 256)
            at_other = pl.ds(pl.multiple_of(256 - y * 256, 256), 256)

            def total(at):
                t = own[k, :, at]
                for j in range(3):
                    t += recv_a[k, j, :, at].astype(F32)
                return t

            send_b[k] = total(at_other)
            copy_b(k).start()
            half[k] = total(at_mine)

        def pack(done, to, rows):
            largest = jnp.max(jnp.max(jnp.abs(done), axis=0, keepdims=True), axis=1, keepdims=True)
            power = jnp.maximum(jnp.ceil(jnp.log2(jnp.maximum(largest, 1e-30))), -99.0)
            steps = jnp.clip(jnp.round(done * jnp.exp2(15.0 - power)), -32767.0, 32767.0)
            to[0:rows, :] = steps.astype(jnp.int32).astype(jnp.int16)
            to[rows : rows + 16, :] = jnp.broadcast_to(power, (16, 256)).astype(jnp.int32).astype(jnp.int16)

        def place(q, values):
            tile[q] = values[:, other_128].T
            copy_t(q, core).start()
            out[:, pl.ds(pl.multiple_of(q * 256 + core * 128, 128), 128)] = values[:, mine_128].T

        def spread(k, done):
            at = pl.ds(pl.multiple_of(k * 16, 16), 16)
            for q in range(8):
                gathered[q, at, :] = done[q * 16 : q * 16 + 16, :]

        def sum_y(k):
            copy_b(k).wait_recv()
            spread(k, (half[k] + recv_b[k]) * NORM)

        def step(k, carry):
            multiply(k)

            @pl.when(k >= 1)
            def _():
                sum_x(k - 1)

            @pl.when(k >= 2)
            def _():
                sum_y(k - 2)

            return carry

        lax.fori_loop(0, LAST, step, 0)
        sum_y(LAST - 2)
        for q in range(8):
            pack(gathered[q, 0:96, :], ret.at[q], 96)

        arrived(LAST)
        for n in range(8):
            return_copy(lax.rem(chip + n, 8)).start()
        for n in (5, 4, 3, 2, 7, 6, 1, 0):
            part = product(pl.ds(pl.multiple_of(chip_at(n // 2, n % 2) * 256, 256), 256))
            if n:
                send_d[n - 1] = part.astype(BF)
                copy_d(n).start()
            else:
                half[LAST] = part
        sum_x(LAST - 1)
        total = half[LAST]
        for n in range(1, 8):
            copy_d(n).wait_recv()
            total += recv_d[n - 1].astype(F32)
        sum_y(LAST - 1)
        spread(LAST, total * NORM)
        for n in range(8):
            q = lax.rem(chip + n, 8)
            pack(gathered[q, 96:128, :], ret_last.at[q], 32)
            return_last(q).start()
        for q in range(8):
            place(q, gathered.at[q])

        def finish(k, carry):
            for j in range(1, 4):
                copy_a(k, j).wait_send()
            copy_b(k).wait_send()
            return carry

        lax.fori_loop(0, LAST, finish, 0)
        for n in range(1, 8):
            copy_d(n).wait_send()
        for q in range(8):
            return_copy(q).wait_send()
            return_last(q).wait_send()
            copy_t(q, core).wait_send()
            copy_t(q, 1 - core).wait_recv()


def shards(design, species, species_weight):
    dma = pltpu.SemaphoreType.DMA
    vmem = pltpu.VMEM
    return pl.pallas_call(
        kernel,
        out_shape=jax.ShapeDtypeStruct((128, WIDTH), F32),
        in_specs=[pl.BlockSpec(memory_space=pltpu.HBM)] * 3,
        out_specs=pl.BlockSpec(memory_space=pltpu.VMEM),
        scratch_shapes=[
            vmem((2, DEPTH, WIDTH), BF),
            vmem((2, DEPTH, 128), F32),
            vmem((2 * DEPTH, WIDTH), BF),
            vmem((2 * DEPTH, WIDTH), BF),
            vmem((NB, 2 * DEPTH, 128), BF),
            vmem((128, 2 * DEPTH), BF),
            vmem((LAST, 3, 128, 512), BF),
            vmem((LAST, 3, 128, 512), BF),
            vmem((LAST, 128, 512), F32),
            vmem((LAST, 128, 256), F32),
            vmem((LAST, 128, 256), F32),
            vmem((NB, 128, 256), F32),
            vmem((8, 112, 256), jnp.int16),
            vmem((NB, 128, 128), F32),
            vmem((NB // 2, 2, DEPTH, 128), BF),
            vmem((8, 160, 256), jnp.int16),
            vmem((DEPTH,), jnp.int32),
            pltpu.SMEM((10,), F32),
            vmem((NB, 2, DEPTH, 128), BF),
            vmem((8, 128, 256), F32),
            vmem((8, 48, 256), jnp.int16),
            vmem((7, 128, 256), BF),
            vmem((7, 128, 256), BF),
            dma((3,)),
            dma, dma, dma, dma,
            dma((NB, 2)), dma((NB, 2)),
            dma((LAST, 3)), dma((LAST, 3)),
            dma((LAST,)), dma((LAST,)),
            dma((NB,)), dma((NB,)),
            dma((8,)), dma((8,)),
            dma((NB // 2, 2)), dma((NB // 2, 2)),
            dma((7,)), dma((7,)),
            dma((8,)), dma((8,)),
        ],
        compiler_params=pltpu.CompilerParams(
            collective_id=0, has_side_effects=True, vmem_limit_bytes=50 * 2**20
        ),
        cost_estimate=pl.CostEstimate(flops=4 * 1536 * 2048 * 1024, bytes_accessed=8 * 2**20, transcendentals=0),
    )(*(pltpu.with_memory_space_constraint(a, pltpu.HBM) for a in (design, species, species_weight)))


def solution(mesh):
    placed = (P("row", "col"), P("row"), P())
    return jax.shard_map(
        shards, mesh=mesh, in_specs=placed, out_specs=P(("col", "row"), None), check_vma=False
    )
```

time: 105 us -> 101 us (0.962)
  the two profiles are of different devices: /device:TPU:95 before, /device:TPU:1 now
where the time goes in v4:
time: 101 us
  Pallas kernels  99.8 us (99%)
    pallas_call x1, Pallas kernels, shards(): pl.pallas_call(kernel, out_shape=jax.ShapeDtypeStruct((128, WIDTH), F32),...  99.8 us

profile of v4, /device:TPU:1, one launch (start us, length us, event | category | flops | bytes accessed | tf_op | source)
XLA Modules:
  0.0 100.8 jit_solution(2090204469186445843)
XLA Ops:
  0.0 99.8 %shard_map.37 = f32[128,2048]{1,0:T(8,128)S(1)} custom-call(bf16[768,2048]{1,0:T(8,128)(2,1)} %design.1, s32[768]{0:T(1024)} %species.1, f32[10]{0:T(128)} %species_weight.1), custom_call_target="tpu_custom_call" | custom-call | flops 12884901888 | bytes 8388608 | tf_op jit(solution)/shard_map/pallas_call | solution.py:311
  99.8 1.0 copy.5

commit v5 on v4

--- a/solution.py
+++ b/solution.py
@@ -18,7 +18,7 @@
 def kernel(
     design, species, species_weight, out,
     raw, wv, hi, lo, rbuf, rt, send_a, recv_a, own, send_b, recv_b, half, ret, tile, stage, recv_q, species_here, weight_here,
-    mix, gathered, ret_last, send_d, recv_d,
+    mix, gathered, ret_last, recv_l, send_d, recv_d,
     local_sem, ls, lr, ws, wr, rs, rr, as_, ar, bs, br, ts, tr, os_, orr, gs, gr, ds_, dr, fs, fr,
 ):
     row = lax.axis_index("row")
@@ -60,10 +60,10 @@
         return copy(stage.at[i, c], rbuf.at[k, my_rows, :], rs.at[k, c], rr.at[k, core], chip * 2 + c, 15 - beside)
 
     def return_copy(q):
-        return copy(ret.at[q], recv_q.at[chip, pl.ds(0, 112), :], os_.at[q], orr.at[chip], 2 * q + core, mirror)
+        return copy(ret.at[q], recv_q.at[chip], os_.at[q], orr.at[chip], 2 * q + core, mirror)
 
     def return_last(q):
-        return copy(ret_last.at[q], recv_q.at[chip, pl.ds(112, 48), :], fs.at[q], fr.at[chip], 2 * q + core, mirror)
+        return copy(ret_last.at[q], recv_l.at[chip], fs.at[q], fr.at[chip], 2 * q + core, mirror)
 
     @pl.when(jnp.logical_not(computes))
     def _():
@@ -113,16 +113,15 @@
         for c in range(2):
             forward_copy(NB // 2 - 1, c).wait_send()
 
-        def unpack(q, rows, first, to):
-            size = jnp.exp2(recv_q[q, first + rows : first + rows + 16, :].astype(F32)[0:1, :] - 15.0)
-            out[to : to + rows, q * 256 : q * 256 + 256] = recv_q[q, first : first + rows, :].astype(F32) * size
-
-        for q in range(8):
-            copy(ret.at[0], recv_q.at[q, pl.ds(0, 112), :], os_.at[0], orr.at[q], row, mirror).wait_recv()
-            unpack(q, 96, 0, 0)
-        for q in range(8):
-            copy(ret_last.at[0], recv_q.at[q, pl.ds(112, 48), :], fs.at[0], fr.at[q], row, mirror).wait_recv()
-            unpack(q, 32, 112, 96)
+        for q in range(8):
+            copy(ret.at[0], recv_q.at[q], os_.at[0], orr.at[q], row, mirror).wait_recv()
+            size = jnp.exp2(recv_q[q, 192:208, :].astype(F32)[0:1, :] - 15.0)
+            for h in range(2):
+                at = q * 256 + h * 128
+                out[0:96, at : at + 128] = recv_q[q, h * 96 : h * 96 + 96, :].astype(F32) * size
+        for q in range(8):
+            copy(ret_last.at[0], recv_l.at[q], fs.at[0], fr.at[q], row, mirror).wait_recv()
+            out[96:128, q * 256 : q * 256 + 256] = recv_l[q].astype(F32)
 
     @pl.when(computes)
     def _():
@@ -226,12 +225,14 @@
             copy_b(k).start()
             half[k] = total(at_mine)
 
-        def pack(done, to, rows):
+        def pack(done, to):
             largest = jnp.max(jnp.max(jnp.abs(done), axis=0, keepdims=True), axis=1, keepdims=True)
             power = jnp.maximum(jnp.ceil(jnp.log2(jnp.maximum(largest, 1e-30))), -99.0)
             steps = jnp.clip(jnp.round(done * jnp.exp2(15.0 - power)), -32767.0, 32767.0)
-            to[0:rows, :] = steps.astype(jnp.int32).astype(jnp.int16)
-            to[rows : rows + 16, :] = jnp.broadcast_to(power, (16, 256)).astype(jnp.int32).astype(jnp.int16)
+            steps = steps.astype(jnp.int32).astype(jnp.int16)
+            to[0:96, :] = steps[:, 0:128]
+            to[96:192, :] = steps[:, 128:256]
+            to[192:208, :] = jnp.broadcast_to(power, (16, 128)).astype(jnp.int32).astype(jnp.int16)
 
         def place(q, values):
             tile[q] = values[:, other_128].T
@@ -263,11 +264,11 @@
         lax.fori_loop(0, LAST, step, 0)
         sum_y(LAST - 2)
         for q in range(8):
-            pack(gathered[q, 0:96, :], ret.at[q], 96)
-
-        arrived(LAST)
+            pack(gathered[q, 0:96, :], ret.at[q])
+
         for n in range(8):
             return_copy(lax.rem(chip + n, 8)).start()
+        arrived(LAST)
         for n in (5, 4, 3, 2, 7, 6, 1, 0):
             part = product(pl.ds(pl.multiple_of(chip_at(n // 2, n % 2) * 256, 256), 256))
             if n:
@@ -284,7 +285,7 @@
         spread(LAST, total * NORM)
         for n in range(8):
             q = lax.rem(chip + n, 8)
-            pack(gathered[q, 96:128, :], ret_last.at[q], 32)
+            ret_last[q] = gathered[q, 96:128, :].astype(BF)
             return_last(q).start()
         for q in range(8):
             place(q, gathered.at[q])
@@ -326,15 +327,16 @@
             vmem((LAST, 128, 256), F32),
             vmem((LAST, 128, 256), F32),
             vmem((NB, 128, 256), F32),
-            vmem((8, 112, 256), jnp.int16),
+            vmem((8, 208, 128), jnp.int16),
             vmem((NB, 128, 128), F32),
             vmem((NB // 2, 2, DEPTH, 128), BF),
-            vmem((8, 160, 256), jnp.int16),
+            vmem((8, 208, 128), jnp.int16),
             vmem((DEPTH,), jnp.int32),
             pltpu.SMEM((10,), F32),
             vmem((NB, 2, DEPTH, 128), BF),
             vmem((8, 128, 256), F32),
-            vmem((8, 48, 256), jnp.int16),
+            vmem((8, 32, 256), BF),
+            vmem((8, 32, 256), BF),
             vmem((7, 128, 256), BF),
             vmem((7, 128, 256), BF),
             dma((3,)),

time: 101 us -> 99.2 us (0.982)
  Pallas kernels: 99.8 us -> 98.1 us
    pallas_call x1, Pallas kernels: 99.8 us -> 98.1 us  [shards(): pl.pallas_call(kernel, out_shape=jax.ShapeDtypeStruct((128, WIDTH), F32),...]
where the time goes in v5:
time: 99.2 us; the launch traced here: 99.1 us
  Pallas kernels  98.1 us (99%)
    pallas_call x1, Pallas kernels, shards(): pl.pallas_call(kernel, out_shape=jax.ShapeDtypeStruct((128, WIDTH), F32),...  98.1 us

profile of v5, /device:TPU:1, one launch (start us, length us, event | category | flops | bytes accessed | tf_op | source)
XLA Modules:
  0.0 99.1 jit_solution(11921164526353214076)
XLA Ops:
  0.0 98.1 %shard_map.37 = f32[128,2048]{1,0:T(8,128)S(1)} custom-call(bf16[768,2048]{1,0:T(8,128)(2,1)} %design.1, s32[768]{0:T(1024)} %species.1, f32[10]{0:T(128)} %species_weight.1), custom_call_target="tpu_custom_call" | custom-call | flops 12884901888 | bytes 8388608 | tf_op jit(solution)/shard_map/pallas_call | solution.py:312
  98.1 1.0 copy.5

commit v6 on v5

--- a/solution.py
+++ b/solution.py
@@ -12,6 +12,7 @@
 WIDTH = 2048
 NB = 8
 LAST = NB - 1
+WINDOW = 2
 NORM = float(12288) ** -0.5
 
 
@@ -83,36 +84,36 @@
                 mix[k, c] = jnp.dot(found, order, preferred_element_type=F32).astype(BF)
             return carry
 
+        sends = [(k, c) for k in range(NB) for c in range(2)]
+
+        def send(k, c):
+            return forward_copy(k // 2, c) if k % 2 else design_copy(k, c)
+
         here.wait()
-        lax.fori_loop(0, 2, mixing, 0)
+        mixing(0, 0)
         pl.semaphore_wait(barrier, 5)
-        for c in range(2):
-            stage_copy(0, c).start()
-        for c in range(2):
-            design_copy(0, c).start()
-        lax.fori_loop(2, 4, mixing, 0)
-        for c in range(2):
-            stage_copy(1, c).start()
-        lax.fori_loop(4, NB, mixing, 0)
-
+        for n, (k, c) in enumerate(sends):
+            if n >= WINDOW:
+                send(*sends[n - WINDOW]).wait_send()
+            if k % 2:
+                stage_copy(k // 2, c).wait_recv()
+            send(k, c).start()
+            if n == 1:
+                mixing(1, 0)
+                for d in range(2):
+                    stage_copy(0, d).start()
+                lax.fori_loop(2, 4, mixing, 0)
+                for d in range(2):
+                    stage_copy(1, d).start()
+                lax.fori_loop(4, NB, mixing, 0)
+            if k in (2, 4) and c == 1:
+                for d in range(2):
+                    stage_copy(k // 2 + 1, d).start()
+        for n in range(len(sends) - WINDOW, len(sends)):
+            send(*sends[n]).wait_send()
         for i in range(NB // 2):
-            if 1 <= i < NB // 2 - 1:
-                for c in range(2):
-                    stage_copy(i + 1, c).start()
-            for c in range(2):
-                stage_copy(i, c).wait_recv()
-                forward_copy(i, c).start()
-            if i < NB // 2 - 1:
-                for c in range(2):
-                    design_copy(2 * i + 2, c).start()
             for c in range(2):
                 stage_copy(i, c).wait_send()
-                design_copy(2 * i, c).wait_send()
-                if i >= 1:
-                    forward_copy(i - 1, c).wait_send()
-        for c in range(2):
-            forward_copy(NB // 2 - 1, c).wait_send()
-
         for q in range(8):
             copy(ret.at[0], recv_q.at[q], os_.at[0], orr.at[q], row, mirror).wait_recv()
             size = jnp.exp2(recv_q[q, 192:208, :].astype(F32)[0:1, :] - 15.0)
@@ -268,6 +269,7 @@
 
         for n in range(8):
             return_copy(lax.rem(chip + n, 8)).start()
+        sum_x(LAST - 1)
         arrived(LAST)
         for n in (5, 4, 3, 2, 7, 6, 1, 0):
             part = product(pl.ds(pl.multiple_of(chip_at(n // 2, n % 2) * 256, 256), 256))
@@ -276,12 +278,11 @@
                 copy_d(n).start()
             else:
                 half[LAST] = part
-        sum_x(LAST - 1)
+        sum_y(LAST - 1)
         total = half[LAST]
         for n in range(1, 8):
             copy_d(n).wait_recv()
             total += recv_d[n - 1].astype(F32)
-        sum_y(LAST - 1)
         spread(LAST, total * NORM)
         for n in range(8):
             q = lax.rem(chip + n, 8)

time: 99.2 us -> 97.9 us (0.987)
  Pallas kernels: 98.1 us -> 96.6 us
    pallas_call x1, Pallas kernels: 98.1 us -> 96.6 us  [shards(): pl.pallas_call(kernel, out_shape=jax.ShapeDtypeStruct((128, WIDTH), F32),...]
where the time goes in v6:
time: 97.9 us; the launch traced here: 97.6 us
  Pallas kernels  96.6 us (99%)
    pallas_call x1, Pallas kernels, shards(): pl.pallas_call(kernel, out_shape=jax.ShapeDtypeStruct((128, WIDTH), F32),...  96.6 us

profile of v6, /device:TPU:1, one launch (start us, length us, event | category | flops | bytes accessed | tf_op | source)
XLA Modules:
  0.0 97.6 jit_solution(4266789534380951511)
XLA Ops:
  0.0 96.6 %shard_map.37 = f32[128,2048]{1,0:T(8,128)S(1)} custom-call(bf16[768,2048]{1,0:T(8,128)(2,1)} %design.1, s32[768]{0:T(1024)} %species.1, f32[10]{0:T(128)} %species_weight.1), custom_call_target="tpu_custom_call" | custom-call | flops 12884901888 | bytes 8388608 | tf_op jit(solution)/shard_map/pallas_call | solution.py:313
  96.6 1.0 copy.5

commit v7 on v6

--- a/solution.py
+++ b/solution.py
@@ -63,8 +63,9 @@
     def return_copy(q):
         return copy(ret.at[q], recv_q.at[chip], os_.at[q], orr.at[chip], 2 * q + core, mirror)
 
-    def return_last(q):
-        return copy(ret_last.at[q], recv_l.at[chip], fs.at[q], fr.at[chip], 2 * q + core, mirror)
+    def return_last(q, h):
+        rows = pl.ds(16 * h, 16)
+        return copy(ret_last.at[q, rows, :], recv_l.at[chip, rows, :], fs.at[q, h], fr.at[chip, h], 2 * q + core, mirror)
 
     @pl.when(jnp.logical_not(computes))
     def _():
@@ -121,7 +122,9 @@
                 at = q * 256 + h * 128
                 out[0:96, at : at + 128] = recv_q[q, h * 96 : h * 96 + 96, :].astype(F32) * size
         for q in range(8):
-            copy(ret_last.at[0], recv_l.at[q], fs.at[0], fr.at[q], row, mirror).wait_recv()
+            for h in range(2):
+                rows = pl.ds(16 * h, 16)
+                copy(ret_last.at[0, rows, :], recv_l.at[q, rows, :], fs.at[0, h], fr.at[q, h], row, mirror).wait_recv()
             out[96:128, q * 256 : q * 256 + 256] = recv_l[q].astype(F32)
 
     @pl.when(computes)
@@ -279,6 +282,10 @@
             else:
                 half[LAST] = part
         sum_y(LAST - 1)
+        for n in range(8):
+            q = lax.rem(chip + n, 8)
+            ret_last[q, 0:16, :] = gathered[q, 96:112, :].astype(BF)
+            return_last(q, 0).start()
         total = half[LAST]
         for n in range(1, 8):
             copy_d(n).wait_recv()
@@ -286,8 +293,8 @@
         spread(LAST, total * NORM)
         for n in range(8):
             q = lax.rem(chip + n, 8)
-            ret_last[q] = gathered[q, 96:128, :].astype(BF)
-            return_last(q).start()
+            ret_last[q, 16:32, :] = gathered[q, 112:128, :].astype(BF)
+            return_last(q, 1).start()
         for q in range(8):
             place(q, gathered.at[q])
 
@@ -302,7 +309,8 @@
             copy_d(n).wait_send()
         for q in range(8):
             return_copy(q).wait_send()
-            return_last(q).wait_send()
+            return_last(q, 0).wait_send()
+            return_last(q, 1).wait_send()
             copy_t(q, core).wait_send()
             copy_t(q, 1 - core).wait_recv()
 
@@ -349,7 +357,7 @@
             dma((8,)), dma((8,)),
             dma((NB // 2, 2)), dma((NB // 2, 2)),
             dma((7,)), dma((7,)),
-            dma((8,)), dma((8,)),
+            dma((8, 2)), dma((8, 2)),
         ],
         compiler_params=pltpu.CompilerParams(
             collective_id=0, has_side_effects=True, vmem_limit_bytes=50 * 2**20

time: 97.9 us -> 97.7 us (level)
  no operation moved by 1% of the time
where the time goes in v7:
time: 97.7 us; the launch traced here: 97.6 us
  Pallas kernels  96.6 us (99%)
    pallas_call x1, Pallas kernels, shards(): pl.pallas_call(kernel, out_shape=jax.ShapeDtypeStruct((128, WIDTH), F32),...  96.6 us

profile of v7, /device:TPU:1, one launch (start us, length us, event | category | flops | bytes accessed | tf_op | source)
XLA Modules:
  0.0 97.6 jit_solution(16116908222690054993)
XLA Ops:
  0.0 96.6 %shard_map.37 = f32[128,2048]{1,0:T(8,128)S(1)} custom-call(bf16[768,2048]{1,0:T(8,128)(2,1)} %design.1, s32[768]{0:T(1024)} %species.1, f32[10]{0:T(128)} %species_weight.1), custom_call_target="tpu_custom_call" | custom-call | flops 12884901888 | bytes 8388608 | tf_op jit(solution)/shard_map/pallas_call | solution.py:321
  96.6 1.0 copy.5

commit v8 on v7

--- a/solution.py
+++ b/solution.py
@@ -75,14 +75,19 @@
         here = pltpu.make_async_copy(design, raw.at[0], local_sem.at[0])
         here.start()
 
-        def mixing(k, carry):
+        def order_of(k):
             a = lax.broadcasted_iota(jnp.int32, (1024, 128), 0)
             b = lax.broadcasted_iota(jnp.int32, (1024, 128), 1)
             wanted = lax.div(b, 16) * 128 + k * 16 + lax.rem(b, 16)
-            order = jnp.where(a == wanted, 1.0, 0.0).astype(BF)
+            return jnp.where(a == wanted, 1.0, 0.0).astype(BF)
+
+        def mix_columns(k, order):
             for c in range(2):
                 found = jnp.concatenate([raw[0, :, q * 256 + c * 128 : q * 256 + c * 128 + 128] for q in range(8)], axis=1)
                 mix[k, c] = jnp.dot(found, order, preferred_element_type=F32).astype(BF)
+
+        def mixing(k, carry):
+            mix_columns(k, order_of(k))
             return carry
 
         sends = [(k, c) for k in range(NB) for c in range(2)]
@@ -90,8 +95,9 @@
         def send(k, c):
             return forward_copy(k // 2, c) if k % 2 else design_copy(k, c)
 
+        first = order_of(0)
         here.wait()
-        mixing(0, 0)
+        mix_columns(0, first)
         pl.semaphore_wait(barrier, 5)
         for n, (k, c) in enumerate(sends):
             if n >= WINDOW:

time: 97.7 us -> 97.7 us (level)
  no operation moved by 1% of the time
where the time goes in v8:
time: 97.7 us; the launch traced here: 97.6 us
  Pallas kernels  96.6 us (99%)
    pallas_call x1, Pallas kernels, shards(): pl.pallas_call(kernel, out_shape=jax.ShapeDtypeStruct((128, WIDTH), F32),...  96.6 us

profile of v8, /device:TPU:1, one launch (start us, length us, event | category | flops | bytes accessed | tf_op | source)
XLA Modules:
  0.0 97.6 jit_solution(8999603912996875621)
XLA Ops:
  0.0 96.6 %shard_map.37 = f32[128,2048]{1,0:T(8,128)S(1)} custom-call(bf16[768,2048]{1,0:T(8,128)(2,1)} %design.1, s32[768]{0:T(1024)} %species.1, f32[10]{0:T(128)} %species_weight.1), custom_call_target="tpu_custom_call" | custom-call | flops 12884901888 | bytes 8388608 | tf_op jit(solution)/shard_map/pallas_call | solution.py:327
  96.6 1.0 copy.5
